TPU v7x, 32 devices: a whole 2x2x4 slice. The times are simulated.
32 devices in a mesh: dom: 2 (over y), grp: 4 (over x, core), tp: 4 (over z).
Axes of the slice: x: 2, y: 2, z: 4, core: 2. Of those that a mesh axis runs over, the one named last changes fastest.
Arguments:
- hidden: bfloat16 [32, 128, 16384], P(('dom', 'grp'), None, 'tp'), parts along dimension 0
- norm_gain: float32 [16384], P('tp'), may hold values from 0.1 to 1.9
- kv_weight: bfloat16 [16384, 8, 256], P('tp'), may hold values from -0.046875 to 0.046875
- dest_slot: int32 [32], P(('dom', 'grp')), parts along dimension 0, may hold values from -1 to 7, as said below
- session_len: int32 [8], P(('dom', 'grp')), parts along dimension 0, may hold values from 129 to 256
- session_start: int32 [8], P(('dom', 'grp')), parts along dimension 0, may hold values from 0 to 16383
Outputs:
- kv_cache: bfloat16 [16, 128, 8, 256], P(('dom', 'grp'), None, 'tp'), parts along dimension 0
There are 2 independent parts, one for each index of `dom`. A program takes and returns all parts, laid end to end along the dimension named above; an argument that names none is the same for every part. Nothing has to cross between parts.
Inputs may be any that keep to these rules, and one draw needn't show every extreme that they name: `dest_slot`: each of the 8 cache blocks is named by exactly one stored slot; the blocks of one owner come from different groups, so a group sends at most one block to each owner; a group stores at most 4 blocks and some group stores exactly 4; -1 marks an empty slot.
All inputs are finite; a program needn't handle non-finite values.
Results may differ from a plain program's by a relative error of at most 0.013.
Values may be sent and summed in bfloat16 or wider, within the bound.
A program may use at most 128 MiB of HBM per device.

v0:
```python
import jax
import jax.numpy as jnp
from jax import lax
from jax.sharding import PartitionSpec as P

HD = 128


epsilon = 1e-05


def rotate_keys(kv, positions):
    half = HD // 2
    steps = jnp.arange(half).astype(jnp.float32)
    freqs = jnp.exp(-jnp.log(jnp.float32(500000.0)) * (2.0 * steps / HD))
    angles = positions.astype(jnp.float32)[:, None] * freqs[None, :]
    cosine = jnp.cos(angles)[:, None, :]
    sine = jnp.sin(angles)[:, None, :]
    first = kv[..., :half]
    second = kv[..., half:HD]
    keys = jnp.concatenate(
        [first * cosine - second * sine, second * cosine + first * sine], axis=-1
    )
    return jnp.concatenate([keys, kv[..., HD:]], axis=-1)


def project(blocks, positions, live, norm_gain, kv_weight):
    count, block_len, width = blocks.shape
    tensor_size = lax.axis_size("tp")
    total_rows = count * block_len
    wide = blocks.reshape(total_rows, width).astype(jnp.float32)
    squares = lax.psum(jnp.sum(wide * wide, axis=1), "tp")
    inverse = lax.rsqrt(squares / (width * tensor_size) + epsilon)
    scaled = (wide * norm_gain[None, :]).astype(jnp.bfloat16)
    heads_here = kv_weight.shape[1] // tensor_size
    summed = lax.psum_scatter(
        jnp.einsum("rd,dhe->hre", scaled, kv_weight, preferred_element_type=jnp.float32).astype(
            jnp.bfloat16
        ),
        "tp",
        scatter_dimension=0,
        tiled=True,
    ).astype(jnp.float32)
    kv_rows = jnp.transpose(summed, (1, 0, 2)) * inverse[:, None, None]
    rotated = rotate_keys(kv_rows, positions.reshape(total_rows))
    masked = jnp.where(live.reshape(total_rows)[:, None, None], rotated, 0.0).astype(jnp.bfloat16)
    return masked.reshape(count, block_len, heads_here, kv_weight.shape[2])


def pick_blocks(arrived, arrived_dest, own_count):
    targets = arrived_dest[:, 0]
    chooser = (targets[None, :] >= 0) & (
        targets[None, :] % own_count == jnp.arange(own_count)[:, None]
    )
    return jnp.einsum(
        "js,sbd->jbd", chooser.astype(jnp.bfloat16), arrived, preferred_element_type=jnp.float32
    ).astype(jnp.bfloat16)


def body(hidden, norm_gain, kv_weight, dest_slot, session_len, session_start):
    groups = lax.axis_size("grp")
    slots, block_len, width = hidden.shape
    own_count = (3 * groups + 7) // 8
    owner_of = jnp.where(dest_slot >= 0, dest_slot // own_count, -1)
    select = owner_of[None, :] == jnp.arange(groups)[:, None]
    sent_dest = jnp.sum(jnp.where(select, dest_slot[None, :], 0), axis=1) + jnp.where(
        jnp.any(select, axis=1), 0, -1
    )
    sent_dest = sent_dest[:, None]
    select_bf = select.astype(jnp.bfloat16)
    token_ids = jnp.arange(block_len)
    packed = jnp.einsum(
        "gs,sbd->gbd", select_bf, hidden, preferred_element_type=jnp.float32
    ).astype(jnp.bfloat16)
    arrived, arrived_dest = (
        lax.all_to_all(packed, "grp", split_axis=0, concat_axis=0, tiled=True),
        lax.all_to_all(sent_dest, "grp", split_axis=0, concat_axis=0, tiled=True),
    )
    blocks = pick_blocks(arrived, arrived_dest, own_count)
    offsets = jnp.arange(own_count)[:, None] * block_len + token_ids[None, :]
    positions = session_start[0] + offsets
    live = offsets < session_len[0]
    return project(blocks, positions, live, norm_gain, kv_weight)


def solution(mesh):
    in_specs = (
        P(("dom", "grp"), None, "tp"),
        P("tp"),
        P("tp", None, None),
        P(("dom", "grp")),
        P(("dom", "grp")),
        P(("dom", "grp")),
    )
    out_specs = P(("dom", "grp"), None, "tp", None)
    return jax.shard_map(body, mesh=mesh, in_specs=in_specs, out_specs=out_specs, check_vma=False)
```

profile of v0, /device:TPU:0, one launch (start us, length us, event | category | flops | bytes accessed | tf_op | source)
XLA Modules:
  0.0 135.6 jit_solution(13509567701180820197)
XLA Ops:
  6.5 0.7 compare_select_fusion.2
  7.2 0.1 fusion.19
  7.3 0.8 select_reduce_fusion
  8.1 0.7 copy.25
  8.8 4.2 %all-to-all-start = ((s32[4,1,1]{2,1,0:T(1,128)}), s32[4,1,1]{2,1,0:T(1,128)S(1)}, u32[]{:S(2)}, u32[]{:S(2)}) async-start(s32[4,1,1]{2,1,0:T(1,128)} %copy.25), calls=%async_computation | async-start | bytes 4096 | tf_op jit(solution)/shard_map/all_to_all | solution.py:77
  13.0 5.9 %convolution_convert_fusion = bf16[4,128,4096]{2,0,1:T(4,128)(2,1)S(1)} fusion(bf16[4,128,4096]{2,1,0:T(8,128)(2,1)} %param.6, s32[4]{0:T(128)S(1)} %compare_select_fusion.2), kind=kOutput, calls=%fused_computation.2 | convolution fusion | flops 18874384 | bytes 8388624 | tf_op jit(solution)/shard_map/gs,sbd->gbd/dot_general | solution.py:72
  18.9 4.3 %copy.27 = bf16[4,128,4096]{2,1,0:T(8,128)(2,1)} copy(bf16[4,128,4096]{2,0,1:T(4,128)(2,1)S(1)} %convolution_convert_fusion) | data formatting | bytes 8388608 | tf_op jit(solution)/shard_map/convert_element_type | solution.py:74
  23.2 0.0 all-to-all-done
  23.2 4.9 %all-to-all-start.1 = ((bf16[4,128,4096]{2,1,0:T(8,128)(2,1)}), bf16[4,128,4096]{2,1,0:T(8,128)(2,1)}, u32[]{:S(2)}, u32[]{:S(2)}) async-start(bf16[4,128,4096]{2,1,0:T(8,128)(2,1)} %copy.27), calls=%async_computation.1 | async-start | bytes 8388608 | tf_op jit(solution)/shard_map/all_to_all | solution.py:76
  28.0 0.2 reduce-scatter.2.cloned.1.call-start
  28.3 0.2 reduce.1
  28.4 47.8 %all-to-all-done.1 = bf16[4,128,4096]{2,1,0:T(8,128)(2,1)} async-done(((bf16[4,128,4096]{2,1,0:T(8,128)(2,1)}), bf16[4,128,4096]{2,1,0:T(8,128)(2,1)}, u32[]{:S(2)}, u32[]{:S(2)}) %all-to-all-start.1) | async-done | bytes 4194336 | tf_op jit(solution)/shard_map/all_to_all | solution.py:76
  76.3 7.0 %multiply_reduce_fusion = (f32[2,128]{0,1:T(8,128)S(1)}, f32[2,128,4096]{2,0,1:T(2,128)S(1)}) fusion(bf16[4,128,4096]{2,1,0:T(8,128)(2,1)} %all-to-all-done.1, pred[4]{0:T(512)(128)(4,1)S(1)} %broadcast_compare_fusion, s32[4]{0:T(128)S(1)} %and_select_fusion), kind=kOutput, calls=%fused_computation.8 | convolution fusion | flops 12582672 | bytes 8389652 | tf_op jit(solution)/shard_map/js,sbd->jbd/dot_general | solution.py:55
  83.3 0.0 copy-start
  83.3 2.4 %copy.29 = f32[2,128,4096]{2,1,0:T(8,128)S(1)} copy(f32[2,128,4096]{2,0,1:T(2,128)S(1)} %get-tuple-element.10) | data formatting | bytes 8388608 | tf_op jit(solution)/shard_map/convert_element_type | solution.py:31
  85.7 0.0 copy-done
  85.7 0.4 fusion.3
  86.1 11.3 %fusion.12 = bf16[8,256,256]{2,1,0:T(8,128)(2,1)} fusion(bf16[4096,8,256]{2,1,0:T(8,128)(2,1)} %param.8, bf16[256,4096]{1,0:T(8,128)(2,1)S(1)} %fusion.3), kind=kOutput, calls=%fused_computation.12 | convolution fusion | flops 4295491584 | bytes 19922944 | tf_op jit(solution)/shard_map/rd,dhe->hre/dot_general | solution.py:37
  97.4 0.0 reduce-scatter.2.cloned.1.call-update
  98.7 0.1 fusion.26
  98.8 0.1 convert_bitcast_fusion
  98.9 0.5 multiply_cosine_fusion
  99.4 0.1 copy.31
  99.5 12.6 %psum.7 = f32[256]{0:T(256)S(1)} all-reduce(f32[256]{0:T(256)S(1)} %bitcast.38), channel_id=1, replica_groups=mesh['dom'=2,'grp'=4,'tp'=4] {'tp'}, use_global_device_ids=true, to_apply=%region_4.5 | all-reduce | flops 256 | bytes 2048 | tf_op jit(solution)/shard_map/psum | solution.py:32
  112.1 13.5 %reduce-scatter.2.cloned.1.call-done = bf16[2,256,256]{2,1,0:T(8,128)(2,1)} async-done(((bf16[8,256,256]{2,1,0:T(8,128)(2,1)}), bf16[2,256,256]{2,1,0:T(8,128)(2,1)}) %reduce-scatter.2.cloned.1.call-update) | async-done | bytes 262160 | tf_op jit(solution)/shard_map/reduce_scatter | solution.py:36
  125.6 1.0 multiply_bitcast_fusion
  126.7 0.2 multiply_subtract_fusion
  126.9 0.1 copy.32
  127.0 0.1 copy.33
  127.1 0.1 copy.34
  127.3 1.5 %fusion.17 = bf16[2,128,2,256]{3,2,1,0:T(2,128)(2,1)} fusion(bf16[2,128,2,128]{3,2,1,0:T(2,128)(2,1)S(1)} %copy.34, bf16[2,128,2,64]{3,2,1,0:T(2,128)(2,1)S(1)} %copy.33, bf16[2,128,2,64]{3,2,1,0:T(2,128)(2,1)S(1)} %copy.32, pred[2,128]{1,0:T(4,128)(4,1)S(1)} %fusion.26), kind=kLoop, calls=%fused_computation.14 | loop fusion | flops 917504 | bytes 524544 | tf_op jit(solution)/shard_map/convert_element_type | solution.py:46
  (7 shorter events, 0.1 us)
Async XLA Ops:
  8.8 14.4 %all-to-all-start = ((s32[4,1,1]{2,1,0:T(1,128)}), s32[4,1,1]{2,1,0:T(1,128)S(1)}, u32[]{:S(2)}, u32[]{:S(2)}) async-start(s32[4,1,1]{2,1,0:T(1,128)} %copy.25), calls=%async_computation | async-start | bytes 4096 | tf_op jit(solution)/shard_map/all_to_all | solution.py:77
  23.2 53.1 %all-to-all-start.1 = ((bf16[4,128,4096]{2,1,0:T(8,128)(2,1)}), bf16[4,128,4096]{2,1,0:T(8,128)(2,1)}, u32[]{:S(2)}, u32[]{:S(2)}) async-start(bf16[4,128,4096]{2,1,0:T(8,128)(2,1)} %copy.27), calls=%async_computation.1 | async-start | bytes 8388608 | tf_op jit(solution)/shard_map/all_to_all | solution.py:76
  28.0 97.6 %reduce-scatter.2.cloned.1.call-start = ((), (), s32[]{:S(2)}) async-start(), calls=%async_computation.3 | async-start | bytes 1310720 | tf_op jit(solution)/shard_map/reduce_scatter | solution.py:36
  83.3 2.5 %copy-start = (f32[4096]{0:T(1024)S(1)}, f32[4096]{0:T(1024)}, u32[]{:S(2)}) copy-start(f32[4096]{0:T(1024)} %param.7) | copy-start | bytes 49156
Sparse Core Ops, SparseCore 0:
  97.5 28.0 reduce-scatter.1
where the time goes:
time: 136 us
  waiting for transfers between devices  61.3 us (45%)
  matrix products  24.2 us (18%)
  between operations  14.8 us (11%)
  blocking collectives  12.6 us (9%)
  starting transfers between devices  9.29 us (7%)
  local copies, waits for them, and re-layouts  7.88 us (6%)
  other arithmetic  5.5 us (4%)
    all_to_all x1, waiting for transfers between devices, body(): lax.all_to_all(packed, 'grp', split_axis=0, concat_axis=0, tiled=True)  47.8 us
    reduce_scatter x1, waiting for transfers between devices, project(): lax.psum_scatter(jnp.einsum('rd,dhe->hre', scaled, kv_weight, preferred_e...  13.5 us
    psum x1, blocking collectives, project(): squares = lax.psum(jnp.sum(wide * wide, axis=1), 'tp')  12.6 us
    dot_general x1, matrix products, project(): jnp.einsum('rd,dhe->hre', scaled, kv_weight, preferred_element_type=jnp.f...  11.3 us
    dot_general x1, matrix products, pick_blocks(): jnp.einsum('js,sbd->jbd', chooser.astype(jnp.bfloat16), arrived, preferre...  7 us
    dot_general x1, matrix products, body(): jnp.einsum('gs,sbd->gbd', select_bf, hidden, preferred_element_type=jnp.f...  5.9 us
    all_to_all x1, starting transfers between devices, body(): lax.all_to_all(packed, 'grp', split_axis=0, concat_axis=0, tiled=True)  4.86 us
    convert_element_type x1, local copies, waits for them, and re-layouts, body(): packed = jnp.einsum('gs,sbd->gbd', select_bf, hidden, preferred_element_t...  4.27 us
  transfers between devices with their start and end apart: 3, of which 2 were waited for; matrix products, arithmetic and copies ran while one was open for 8% of the time, Pallas kernels for 0%

commit v1 on v0

v1 whole, which is shorter than its diff:
```python
import functools

import jax
import jax.numpy as jnp
from jax import lax
from jax.experimental import pallas as pl
from jax.experimental.pallas import tpu as pltpu
from jax.sharding import PartitionSpec as P

HD = 128
epsilon = 1e-05
MESH = pl.DeviceIdType.MESH


def exchange_kernel(
    groups, tps, own, heads, width,
    dest_ref, len_ref, part_ref, ss_ref, cos_ref, sin_ref,
    out_ref,
    sent, got, mixed, final, meta_s, meta_r, sums_s, sums_r,
    s_send, s_recv, c_send, c_recv, m_send, m_recv, q_send, q_recv,
):
    g = lax.axis_index("grp")
    z = lax.axis_index("tp")
    slots = part_ref.shape[1]
    blk = part_ref.shape[2]
    wide = part_ref.shape[3]

    def over(n, body):
        lax.fori_loop(0, n, lambda i, c: (body(i), c)[1], 0)

    def grp_peer(k):
        return lax.rem(g + k + 1, groups)

    def tp_peer(k):
        return lax.rem(z + k + 1, tps)

    barrier = pltpu.get_barrier_semaphore()

    @functools.partial(over, groups - 1)
    def _(k):
        pl.semaphore_signal(barrier, inc=1, device_id={"grp": grp_peer(k)}, device_id_type=MESH)

    @functools.partial(over, tps - 1)
    def _(k):
        pl.semaphore_signal(barrier, inc=1, device_id={"tp": tp_peer(k)}, device_id_type=MESH)

    def slot_of(owner):
        index, code = jnp.int32(0), jnp.int32(0)
        for s in range(slots):
            inner = dest_ref[s] - owner * own
            hit = (inner >= 0) & (inner < own)
            index = jnp.where(hit, s, index)
            code = jnp.where(hit, inner + 1, code)
        return index, code

    rows8 = lax.broadcasted_iota(jnp.int32, (8, wide), 0)

    def meta_of(owner):
        index, code = slot_of(owner)
        squares = jnp.broadcast_to(ss_ref[index], (8, wide))
        marks = jnp.full((8, wide), code.astype(jnp.float32))
        return jnp.where(rows8 == 0, squares, marks)

    def block_copy(t, o, src_g):
        return pltpu.make_async_remote_copy(
            src_ref=sent.at[t, o], dst_ref=got.at[t, src_g],
            send_sem=s_send.at[t, o], recv_sem=s_recv.at[t, src_g],
            device_id={"grp": o}, device_id_type=MESH,
        )

    def meta_copy(o, src_g):
        return pltpu.make_async_remote_copy(
            src_ref=meta_s.at[o], dst_ref=meta_r.at[src_g],
            send_sem=m_send.at[o], recv_sem=m_recv.at[src_g],
            device_id={"grp": o}, device_id_type=MESH,
        )

    def shard_copy(t, src_z):
        return pltpu.make_async_remote_copy(
            src_ref=mixed.at[t], dst_ref=final.at[src_z],
            send_sem=c_send.at[t], recv_sem=c_recv.at[src_z],
            device_id={"tp": t}, device_id_type=MESH,
        )

    def sums_copy(t, src_z):
        return pltpu.make_async_remote_copy(
            src_ref=sums_s, dst_ref=sums_r.at[src_z],
            send_sem=q_send.at[t], recv_sem=q_recv.at[src_z],
            device_id={"tp": t}, device_id_type=MESH,
        )

    meta_r[g] = meta_of(g)

    @functools.partial(over, groups - 1)
    def _(k):
        o = grp_peer(k)
        meta_s[o] = meta_of(o)

    pl.semaphore_wait(barrier, groups + tps - 2)

    @functools.partial(over, groups - 1)
    def _(k):
        meta_copy(grp_peer(k), g).start()

    @functools.partial(over, tps)
    def _(i):
        t = tp_peer(i)

        @functools.partial(over, groups - 1)
        def _(k):
            o = grp_peer(k)
            index, _ = slot_of(o)
            for h in range(heads):
                sent[t, o, h] = part_ref[t * heads + h, index]
            block_copy(t, o, g).start()

        mine, _ = slot_of(g)
        for h in range(heads):
            got[t, g, h] = part_ref[t * heads + h, mine]

    @functools.partial(over, groups - 1)
    def _(k):
        o = grp_peer(k)
        meta_copy(o, o).wait_recv()

    def add_squares(s, total):
        marks = jnp.broadcast_to(meta_r[s, 1:2, :], (8, wide))
        squares = jnp.broadcast_to(meta_r[s, 0:1, :], (8, wide))
        return total + jnp.where(marks == (rows8 + 1).astype(jnp.float32), squares, 0.0)

    sums = lax.fori_loop(0, groups, add_squares, jnp.zeros((8, wide), jnp.float32))
    sums_s[...] = sums

    @functools.partial(over, tps - 1)
    def _(i):
        sums_copy(tp_peer(i), z).start()

    def mix(t):
        @functools.partial(over, groups - 1)
        def _(k):
            o = grp_peer(k)
            block_copy(t, o, o).wait_recv()

        for j in range(own):
            for h in range(heads):
                def pick(s, total):
                    marks = jnp.broadcast_to(meta_r[s, 1:2, :], (blk, wide))
                    block = got[t, s, h].astype(jnp.float32)
                    return total + jnp.where(marks == float(j + 1), block, 0.0)

                picked = lax.fori_loop(0, groups, pick, jnp.zeros((blk, wide), jnp.float32))
                mixed[t, j, h] = picked.astype(jnp.bfloat16)

    @functools.partial(over, tps - 1)
    def _(i):
        t = tp_peer(i)
        mix(t)
        shard_copy(t, z).start()

    mix(z)

    @functools.partial(over, tps - 1)
    def _(i):
        t = tp_peer(i)
        sums_copy(t, t).wait_recv()

    def add_sums(i, total):
        return total + sums_r[tp_peer(i)]

    total = lax.fori_loop(0, tps - 1, add_sums, sums)
    inverse = lax.rsqrt(total[:, :blk] / (width * tps) + epsilon)

    @functools.partial(over, tps - 1)
    def _(i):
        t = tp_peer(i)
        shard_copy(t, t).wait_recv()

    half = HD // 2
    token = lax.broadcasted_iota(jnp.int32, (blk, HD), 0)
    length = len_ref[0]
    for j in range(own):
        scale = jnp.transpose(jnp.broadcast_to(inverse[j : j + 1, :], (blk, blk)))
        live = token + j * blk < length
        for h in range(heads):
            def add(i, total):
                return total + final[tp_peer(i), j, h].astype(jnp.float32)

            raw = lax.fori_loop(0, tps - 1, add, mixed[z, j, h].astype(jnp.float32))
            key = raw[:, :HD] * scale
            value = raw[:, HD:] * scale
            swapped = pltpu.roll(key, half, 1)
            turned = key * cos_ref[j] + swapped * sin_ref[j]
            out_ref[j, h, :, :HD] = jnp.where(live, turned, 0.0).astype(out_ref.dtype)
            out_ref[j, h, :, HD:] = jnp.where(live, value, 0.0).astype(out_ref.dtype)

    @functools.partial(over, groups - 1)
    def _(k):
        o = grp_peer(k)
        meta_copy(o, g).wait_send()

    @functools.partial(over, tps)
    def _(t):
        @functools.partial(over, groups - 1)
        def _(k):
            block_copy(t, grp_peer(k), g).wait_send()

    @functools.partial(over, tps - 1)
    def _(i):
        t = tp_peer(i)
        sums_copy(t, z).wait_send()
        shard_copy(t, z).wait_send()


def rotation(start, own, blk):
    half = HD // 2
    steps = jnp.arange(half).astype(jnp.float32)
    freqs = jnp.exp(-jnp.log(jnp.float32(500000.0)) * (2.0 * steps / HD))
    positions = start[0] + jnp.arange(own * blk)
    angles = positions.astype(jnp.float32)[:, None] * freqs[None, :]
    cosine, sine = jnp.cos(angles), jnp.sin(angles)
    return (
        jnp.concatenate([cosine, cosine], axis=1).reshape(own, blk, HD),
        jnp.concatenate([-sine, sine], axis=1).reshape(own, blk, HD),
    )


def body(hidden, norm_gain, kv_weight, dest_slot, session_len, session_start):
    groups, tps = lax.axis_size("grp"), lax.axis_size("tp")
    slots, blk, width = hidden.shape
    own = (3 * groups + 7) // 8
    heads = kv_weight.shape[1] // tps
    wide_cols = kv_weight.shape[2]
    cosine, sine = rotation(session_start, own, blk)
    wide = hidden.astype(jnp.float32)
    squares = jnp.sum(wide * wide, axis=2)
    squares = jnp.concatenate([squares, squares], axis=1)[:, None, :]
    scaled = (wide * norm_gain[None, None, :]).astype(jnp.bfloat16).reshape(slots * blk, width)
    parts = jnp.einsum("rd,dhe->hre", scaled, kv_weight, preferred_element_type=jnp.float32)
    parts = parts.astype(jnp.bfloat16).reshape(kv_weight.shape[1], slots, blk, wide_cols)
    vmem = pl.BlockSpec(memory_space=pltpu.VMEM)
    smem = pl.BlockSpec(memory_space=pltpu.SMEM)
    shard = (heads, blk, wide_cols)
    dma = pltpu.SemaphoreType.DMA
    out = pl.pallas_call(
        functools.partial(exchange_kernel, groups, tps, own, heads, width),
        out_shape=jax.ShapeDtypeStruct((own,) + shard, jnp.bfloat16),
        in_specs=[smem, smem, vmem, vmem, vmem, vmem],
        out_specs=vmem,
        scratch_shapes=[
            pltpu.VMEM((tps, groups) + shard, jnp.bfloat16),
            pltpu.VMEM((tps, groups) + shard, jnp.bfloat16),
            pltpu.VMEM((tps, own) + shard, jnp.bfloat16),
            pltpu.VMEM((tps, own) + shard, jnp.bfloat16),
            pltpu.VMEM((groups, 8, wide_cols), jnp.float32),
            pltpu.VMEM((groups, 8, wide_cols), jnp.float32),
            pltpu.VMEM((8, wide_cols), jnp.float32),
            pltpu.VMEM((tps, 8, wide_cols), jnp.float32),
            dma((tps, groups)), dma((tps, groups)),
            dma((tps,)), dma((tps,)),
            dma((groups,)), dma((groups,)),
            dma((tps,)), dma((tps,)),
        ],
        compiler_params=pltpu.CompilerParams(
            collective_id=0, has_side_effects=True, vmem_limit_bytes=40 * 1024 * 1024
        ),
        name="exchange",
    )(dest_slot, session_len, parts, squares, cosine, sine)
    return jnp.transpose(out, (0, 2, 1, 3))


def solution(mesh):
    in_specs = (
        P(("dom", "grp"), None, "tp"),
        P("tp"),
        P("tp", None, None),
        P(("dom", "grp")),
        P(("dom", "grp")),
        P(("dom", "grp")),
    )
    out_specs = P(("dom", "grp"), None, "tp", None)
    return jax.shard_map(body, mesh=mesh, in_specs=in_specs, out_specs=out_specs, check_vma=False)
```

time: 136 us -> 57.7 us (0.42)
  waiting for transfers between devices: 61.3 us -> 0 us
  Pallas kernels: 0 us -> 38.1 us
  between operations: 14.8 us -> 1.38 us
  blocking collectives: 12.6 us -> 0 us
  matrix products: 24.2 us -> 12.5 us
  starting transfers between devices: 9.29 us -> 0 us
  local copies, waits for them, and re-layouts: 7.88 us -> 0.98 us
    all_to_all x2 -> x0, waiting for transfers between devices: 47.8 us -> none  [the longest x1 47.8 us: body(): lax.all_to_all(packed, 'grp', split_axis=0, concat_axis=0, tiled=True)]
    pallas_call x0 -> x1, Pallas kernels: none -> 38.1 us  [body(): pl.pallas_call(functools.partial(exchange_kernel, groups, tps, own, heads...]
    reduce_scatter x1 -> x0, waiting for transfers between devices: 13.5 us -> none  [project(): lax.psum_scatter(jnp.einsum('rd,dhe->hre', scaled, kv_weight, preferred_e...]
    psum x1 -> x0, blocking collectives: 12.6 us -> none  [project(): squares = lax.psum(jnp.sum(wide * wide, axis=1), 'tp')]
    dot_general x3 -> x1, matrix products: 24.2 us -> 12.5 us  [body(): jnp.einsum('rd,dhe->hre', scaled, kv_weight, preferred_element_type=jnp.f...]
    all_to_all x2 -> x0, starting transfers between devices: 9.07 us -> none  [the longest x1 4.86 us: body(): lax.all_to_all(packed, 'grp', split_axis=0, concat_axis=0, tiled=True)]
    convert_element_type x2 -> x0, local copies, waits for them, and re-layouts: 6.71 us -> none  [the longest x1 4.27 us: body(): packed = jnp.einsum('gs,sbd->gbd', select_bf, hidden, preferred_element_t...]
    reduce_sum x1, other arithmetic: 0.77 us -> 3.85 us  [body(): squares = jnp.sum(wide * wide, axis=2)]
  transfers between devices with their start and end apart: 3 -> 0, of which waited for: 2 -> 0; matrix products, arithmetic and copies ran while one was open for 8% -> 0% of each run, Pallas kernels for 0% -> 0%
where the time goes in v1:
time: 57.7 us; the launch traced here: 57.5 us
  Pallas kernels  38.1 us (66%)
  matrix products  12.5 us (22%)
  other arithmetic  4.54 us (8%)
  between operations  1.38 us (2%)
  local copies, waits for them, and re-layouts  0.98 us (2%)
    pallas_call x1, Pallas kernels, body(): pl.pallas_call(functools.partial(exchange_kernel, groups, tps, own, heads...  38.1 us
    dot_general x1, matrix products, body(): jnp.einsum('rd,dhe->hre', scaled, kv_weight, preferred_element_type=jnp.f...  12.5 us
    reduce_sum x1, other arithmetic, body(): squares = jnp.sum(wide * wide, axis=2)  3.85 us

profile of v1, /device:TPU:0, one launch (start us, length us, event | category | flops | bytes accessed | tf_op | source)
XLA Modules:
  0.0 57.5 jit_solution(17454200820337876951)
XLA Ops:
  0.7 3.8 %fusion.3 = (f32[4,128]{1,0:T(4,128)S(1)}, bf16[4,128,4096]{2,1,0:T(8,128)(2,1)S(1)}) fusion(bf16[4,128,4096]{2,1,0:T(8,128)(2,1)} %param.6, f32[4096]{0:T(1024)} %param.7), kind=kLoop, calls=%fused_computation.5 | loop fusion | flops 10485248 | bytes 8407040 | tf_op jit(solution)/shard_map/reduce_sum | solution.py:235
  4.5 0.0 copy-start
  4.5 12.5 %fusion.4 = bf16[512,8,256]{2,0,1:T(8,128)(2,1)S(1)} fusion(bf16[512,4096,1]{1,0,2:T(8,128)(2,1)S(1)} %bitcast.12, bf16[4096,8,256]{2,1,0:T(8,128)(2,1)} %param.8), kind=kOutput, calls=%fused_computation.6 | convolution fusion | flops 8590983168 | bytes 23068672 | tf_op jit(solution)/shard_map/rd,dhe->hre/dot_general | solution.py:238
  17.7 0.5 fusion.7
  18.3 0.1 pad_maximum_fusion
  18.4 0.0 copy-done
  18.4 38.1 %exchange.1 = bf16[2,2,128,256]{3,2,1,0:T(8,128)(2,1)S(1)} custom-call(s32[4]{0:T(128)S(1)} %copy-done, s32[1]{0:T(128)S(6)} %copy.13.len_ref, bf16[8,4,128,256]{3,2,1,0:T(8,128)(2,1)S(1)} %bitcast.10, f32[4,1,256]{2,1,0:T(1,128)S(1)} %broadcast_in_dim.2.ss_ref, f32[2,128,128]{2,1,0:T(8,128)S(1)} %get-tuple-element.10.cos_ref, ...), custom_call_target="tpu_custom_call" | custom-call | tf_op jit(solution)/shard_map/exchange/pallas_call | solution.py:244
  56.5 1.0 %copy.8 = bf16[2,128,2,256]{3,2,1,0:T(2,128)(2,1)} copy(bf16[2,128,2,256]{3,1,2,0:T(8,128)(2,1)S(1)} %bitcast.11) | data formatting | bytes 524288 | tf_op jit(solution)/shard_map/transpose | solution.py:268
  (4 shorter events, 0.0 us)
Async XLA Ops:
  4.5 13.9 %copy-start = (s32[4]{0:T(128)S(1)}, s32[4]{0:T(128)}, u32[]{:S(2)}) copy-start(s32[4]{0:T(128)} %dest_ref.1) | copy-start | bytes 52

commit v2 on v1

v2 whole, which is shorter than its diff:
```python
import functools

import jax
import jax.numpy as jnp
from jax import lax
from jax.experimental import pallas as pl
from jax.experimental.pallas import tpu as pltpu
from jax.sharding import PartitionSpec as P

HD = 128
epsilon = 1e-05
MESH = pl.DeviceIdType.MESH


def exchange_kernel(
    groups, tps, own, heads, width,
    dest_ref, len_ref, part_ref, hidden_ref, cos_ref, sin_ref,
    out_ref,
    sent, got, mixed, final, mark_s, mark_r, square_s, square_r, sums_s, sums_r, slot_sums, scales,
    s_send, s_recv, c_send, c_recv, m_send, m_recv, r_send, r_recv, q_send, q_recv,
):
    g = lax.axis_index("grp")
    z = lax.axis_index("tp")
    slots = part_ref.shape[1]
    blk = part_ref.shape[2]
    wide = part_ref.shape[3]
    units = sent.shape[1]
    cuts = units // heads
    rows = blk // cuts

    def over(n, body):
        lax.fori_loop(0, n, lambda i, c: (body(i), c)[1], 0)

    def grp_peer(k):
        return lax.rem(g + k + 1, groups)

    def tp_peer(k):
        side = lax.div(k + 1, 2) * (2 * lax.rem(k, 2) - 1)
        return lax.rem(z + tps // 2 + side, tps)

    barrier = pltpu.get_barrier_semaphore()

    @functools.partial(over, groups - 1)
    def _(k):
        pl.semaphore_signal(barrier, inc=1, device_id={"grp": grp_peer(k)}, device_id_type=MESH)

    @functools.partial(over, tps - 1)
    def _(k):
        pl.semaphore_signal(barrier, inc=1, device_id={"tp": tp_peer(k)}, device_id_type=MESH)

    def slot_of(owner):
        index, code = jnp.int32(0), jnp.int32(0)
        for s in range(slots):
            inner = dest_ref[s] - owner * own
            hit = (inner >= 0) & (inner < own)
            index = jnp.where(hit, s, index)
            code = jnp.where(hit, inner + 1, code)
        return index, code

    rows8 = lax.broadcasted_iota(jnp.int32, (8, wide), 0)

    def mark_of(owner):
        _, code = slot_of(owner)
        return jnp.full((8, wide), code.astype(jnp.float32))

    def block_copy(t, u, o, src_g):
        return pltpu.make_async_remote_copy(
            src_ref=sent.at[t, u, o], dst_ref=got.at[t, u, src_g],
            send_sem=s_send.at[t, u, o], recv_sem=s_recv.at[t, u, src_g],
            device_id={"grp": o}, device_id_type=MESH,
        )

    def mark_copy(o, src_g):
        return pltpu.make_async_remote_copy(
            src_ref=mark_s.at[o], dst_ref=mark_r.at[src_g],
            send_sem=m_send.at[o], recv_sem=m_recv.at[src_g],
            device_id={"grp": o}, device_id_type=MESH,
        )

    def square_copy(o, src_g):
        return pltpu.make_async_remote_copy(
            src_ref=square_s.at[o], dst_ref=square_r.at[src_g],
            send_sem=r_send.at[o], recv_sem=r_recv.at[src_g],
            device_id={"grp": o}, device_id_type=MESH,
        )

    def shard_copy(t, u, src_z):
        return pltpu.make_async_remote_copy(
            src_ref=mixed.at[t, u], dst_ref=final.at[src_z, u],
            send_sem=c_send.at[t, u], recv_sem=c_recv.at[src_z, u],
            device_id={"tp": t}, device_id_type=MESH,
        )

    def sums_copy(t, src_z):
        return pltpu.make_async_remote_copy(
            src_ref=sums_s, dst_ref=sums_r.at[src_z],
            send_sem=q_send.at[t], recv_sem=q_recv.at[src_z],
            device_id={"tp": t}, device_id_type=MESH,
        )

    mark_r[g] = mark_of(g)

    @functools.partial(over, groups - 1)
    def _(k):
        o = grp_peer(k)
        mark_s[o] = mark_of(o)

    pl.semaphore_wait(barrier, groups + tps - 2)

    @functools.partial(over, groups - 1)
    def _(k):
        mark_copy(grp_peer(k), g).start()

    mine, _ = slot_of(g)

    @functools.partial(over, tps)
    def _(i):
        t = tp_peer(i)

        @functools.partial(over, units)
        def _(u):
            head = t * heads + lax.div(u, cuts)
            span = pl.ds(pl.multiple_of(lax.rem(u, cuts) * rows, rows), rows)

            @functools.partial(over, groups - 1)
            def _(k):
                o = grp_peer(k)
                index, _ = slot_of(o)
                sent[t, u, o] = part_ref[head, index, span, :]
                block_copy(t, u, o, g).start()

            got[t, u, g] = part_ref[head, mine, span, :]

    @functools.partial(over, groups - 1)
    def _(k):
        o = grp_peer(k)
        mark_copy(o, o).wait_recv()

    def mix(t, u):
        @functools.partial(over, groups - 1)
        def _(k):
            o = grp_peer(k)
            block_copy(t, u, o, o).wait_recv()

        for j in range(own):
            def pick(s, total):
                marks = jnp.broadcast_to(mark_r[s, 0:1, :], (rows, wide))
                block = got[t, u, s].astype(jnp.float32)
                return total + jnp.where(marks == float(j + 1), block, 0.0)

            picked = lax.fori_loop(0, groups, pick, jnp.zeros((rows, wide), jnp.float32))
            mixed[t, u, j] = picked.astype(jnp.bfloat16)

    def mix_and_send(t):
        @functools.partial(over, units)
        def _(u):
            mix(t, u)
            shard_copy(t, u, z).start()

    mix_and_send(tp_peer(0))

    lanes = HD

    @functools.partial(over, slots)
    def _(s):
        for r in range(0, blk, 32):
            def add(c, total):
                span = pl.ds(pl.multiple_of(c * lanes, lanes), lanes)
                x = hidden_ref[s, r : r + 32, span].astype(jnp.float32)
                return total + x * x

            slot_sums[s, r : r + 32, :] = lax.fori_loop(
                0, width // lanes, add, jnp.zeros((32, lanes), jnp.float32)
            )

    def squares_of(owner):
        index, _ = slot_of(owner)
        line = jnp.sum(jnp.transpose(slot_sums[index]), axis=0, keepdims=True)
        return jnp.broadcast_to(jnp.concatenate([line, line], axis=1), (8, wide))

    square_r[g] = squares_of(g)

    @functools.partial(over, groups - 1)
    def _(k):
        o = grp_peer(k)
        square_s[o] = squares_of(o)
        square_copy(o, g).start()

    @functools.partial(over, groups - 1)
    def _(k):
        o = grp_peer(k)
        square_copy(o, o).wait_recv()

    def add_squares(s, total):
        same = mark_r[s] == (rows8 + 1).astype(jnp.float32)
        return total + jnp.where(same, square_r[s], 0.0)

    sums = lax.fori_loop(0, groups, add_squares, jnp.zeros((8, wide), jnp.float32))
    sums_s[...] = sums

    @functools.partial(over, tps - 1)
    def _(i):
        sums_copy(tp_peer(i), z).start()

    @functools.partial(over, tps - 2)
    def _(i):
        mix_and_send(tp_peer(i + 1))

    @functools.partial(over, units)
    def _(u):
        mix(z, u)

    @functools.partial(over, tps - 1)
    def _(i):
        t = tp_peer(i)
        sums_copy(t, t).wait_recv()

    def add_sums(i, total):
        return total + sums_r[tp_peer(i)]

    total = lax.fori_loop(0, tps - 1, add_sums, sums)
    inverse = lax.rsqrt(total[:, :blk] / (width * tps) + epsilon)

    half = HD // 2
    token = lax.broadcasted_iota(jnp.int32, (rows, HD), 0)
    length = len_ref[0]
    for j in range(own):
        scales[j] = jnp.transpose(jnp.broadcast_to(inverse[j : j + 1, :], (blk, blk)))

    @functools.partial(over, units)
    def _(u):
        @functools.partial(over, tps - 1)
        def _(i):
            t = tp_peer(i)
            shard_copy(t, u, t).wait_recv()

        head = lax.div(u, cuts)
        first = pl.multiple_of(lax.rem(u, cuts) * rows, rows)
        span = pl.ds(first, rows)
        for j in range(own):
            live = token + (j * blk + first) < length

            def add(i, total):
                return total + final[tp_peer(i), u, j].astype(jnp.float32)

            raw = lax.fori_loop(0, tps - 1, add, mixed[z, u, j].astype(jnp.float32))
            scale = scales[j, span, :]
            key = raw[:, :HD] * scale
            value = raw[:, HD:] * scale
            swapped = pltpu.roll(key, half, 1)
            turned = key * cos_ref[j, span, :] + swapped * sin_ref[j, span, :]
            out_ref[j, head, span, :HD] = jnp.where(live, turned, 0.0).astype(out_ref.dtype)
            out_ref[j, head, span, HD:] = jnp.where(live, value, 0.0).astype(out_ref.dtype)

    @functools.partial(over, groups - 1)
    def _(k):
        o = grp_peer(k)
        mark_copy(o, g).wait_send()
        square_copy(o, g).wait_send()

    @functools.partial(over, tps)
    def _(t):
        @functools.partial(over, units)
        def _(u):
            @functools.partial(over, groups - 1)
            def _(k):
                block_copy(t, u, grp_peer(k), g).wait_send()

    @functools.partial(over, tps - 1)
    def _(i):
        t = tp_peer(i)
        sums_copy(t, z).wait_send()

        @functools.partial(over, units)
        def _(u):
            shard_copy(t, u, z).wait_send()


def rotation(start, own, blk):
    half = HD // 2
    steps = jnp.arange(half).astype(jnp.float32)
    freqs = jnp.exp(-jnp.log(jnp.float32(500000.0)) * (2.0 * steps / HD))
    positions = start[0] + jnp.arange(own * blk)
    angles = positions.astype(jnp.float32)[:, None] * freqs[None, :]
    cosine, sine = jnp.cos(angles), jnp.sin(angles)
    return (
        jnp.concatenate([cosine, cosine], axis=1).reshape(own, blk, HD),
        jnp.concatenate([-sine, sine], axis=1).reshape(own, blk, HD),
    )


def body(hidden, norm_gain, kv_weight, dest_slot, session_len, session_start):
    groups, tps = lax.axis_size("grp"), lax.axis_size("tp")
    slots, blk, width = hidden.shape
    own = (3 * groups + 7) // 8
    heads = kv_weight.shape[1] // tps
    wide_cols = kv_weight.shape[2]
    cosine, sine = rotation(session_start, own, blk)
    wide = hidden.astype(jnp.float32)
    scaled = (wide * norm_gain[None, None, :]).astype(jnp.bfloat16).reshape(slots * blk, width)
    parts = jnp.einsum("rd,dhe->hre", scaled, kv_weight, preferred_element_type=jnp.float32)
    parts = parts.astype(jnp.bfloat16).reshape(kv_weight.shape[1], slots, blk, wide_cols)
    vmem = pl.BlockSpec(memory_space=pltpu.VMEM)
    smem = pl.BlockSpec(memory_space=pltpu.SMEM)
    cuts = 2
    units = heads * cuts
    piece = (blk // cuts, wide_cols)
    line = pltpu.VMEM((groups, 8, wide_cols), jnp.float32)
    dma = pltpu.SemaphoreType.DMA
    out = pl.pallas_call(
        functools.partial(exchange_kernel, groups, tps, own, heads, width),
        out_shape=jax.ShapeDtypeStruct((own, heads, blk, wide_cols), jnp.bfloat16),
        in_specs=[smem, smem, vmem, vmem, vmem, vmem],
        out_specs=vmem,
        scratch_shapes=[
            pltpu.VMEM((tps, units, groups) + piece, jnp.bfloat16),
            pltpu.VMEM((tps, units, groups) + piece, jnp.bfloat16),
            pltpu.VMEM((tps, units, own) + piece, jnp.bfloat16),
            pltpu.VMEM((tps, units, own) + piece, jnp.bfloat16),
            line, line, line, line,
            pltpu.VMEM((8, wide_cols), jnp.float32),
            pltpu.VMEM((tps, 8, wide_cols), jnp.float32),
            pltpu.VMEM((slots, blk, HD), jnp.float32),
            pltpu.VMEM((own, blk, HD), jnp.float32),
            dma((tps, units, groups)), dma((tps, units, groups)),
            dma((tps, units)), dma((tps, units)),
            dma((groups,)), dma((groups,)),
            dma((groups,)), dma((groups,)),
            dma((tps,)), dma((tps,)),
        ],
        compiler_params=pltpu.CompilerParams(
            collective_id=0, has_side_effects=True, vmem_limit_bytes=40 * 1024 * 1024
        ),
        name="exchange",
    )(dest_slot, session_len, parts, hidden, cosine, sine)
    return jnp.transpose(out, (0, 2, 1, 3))


def solution(mesh):
    in_specs = (
        P(("dom", "grp"), None, "tp"),
        P("tp"),
        P("tp", None, None),
        P(("dom", "grp")),
        P(("dom", "grp")),
        P(("dom", "grp")),
    )
    out_specs = P(("dom", "grp"), None, "tp", None)
    return jax.shard_map(body, mesh=mesh, in_specs=in_specs, out_specs=out_specs, check_vma=False)
```

time: 57.7 us -> 66.1 us (1.15)
  Pallas kernels: 38.1 us -> 47.2 us
  other arithmetic: 4.54 us -> 3.74 us
    pallas_call x1, Pallas kernels: 38.1 us -> 47.2 us  [body(): pl.pallas_call(functools.partial(exchange_kernel, groups, tps, own, heads...]
    reduce_sum x1 -> x0, other arithmetic: 3.85 us -> none  [body(): squares = jnp.sum(wide * wide, axis=2)]
    convert_element_type x0 -> x1, other arithmetic: none -> 3.05 us  [body(): (wide * norm_gain[None, None, :]).astype(jnp.bfloat16)]
where the time goes in v2:
time: 66.1 us; the launch traced here: 65.9 us
  Pallas kernels  47.2 us (71%)
  matrix products  12.7 us (19%)
  other arithmetic  3.74 us (6%)
  between operations  1.38 us (2%)
  local copies, waits for them, and re-layouts  0.99 us (1%)
    pallas_call x1, Pallas kernels, body(): pl.pallas_call(functools.partial(exchange_kernel, groups, tps, own, heads...  47.2 us
    dot_general x1, matrix products, body(): jnp.einsum('rd,dhe->hre', scaled, kv_weight, preferred_element_type=jnp.f...  12.7 us
    convert_element_type x1, other arithmetic, body(): (wide * norm_gain[None, None, :]).astype(jnp.bfloat16)  3.05 us

profile of v2, /device:TPU:0, one launch (start us, length us, event | category | flops | bytes accessed | tf_op | source)
XLA Modules:
  0.0 65.9 jit_solution(6050629952502693261)
XLA Ops:
  0.7 3.1 %multiply_convert_fusion = bf16[4,128,4096]{2,1,0:T(8,128)(2,1)S(1)} fusion(bf16[4,128,4096]{2,1,0:T(8,128)(2,1)} %hidden_ref.1, f32[4096]{0:T(1024)} %param.7), kind=kLoop, calls=%fused_computation.2 | loop fusion | flops 6291456 | bytes 8404992 | tf_op jit(solution)/shard_map/convert_element_type | solution.py:300
  3.7 0.0 copy-start
  3.7 0.0 copy-start.1
  3.7 12.7 %fusion.2 = bf16[512,8,256]{2,0,1:T(8,128)(2,1)S(1)} fusion(bf16[512,4096,1]{1,0,2:T(8,128)(2,1)S(1)} %bitcast.12, bf16[4096,8,256]{2,1,0:T(8,128)(2,1)} %param.8), kind=kOutput, calls=%fused_computation.3 | convolution fusion | flops 8590983168 | bytes 23068672 | tf_op jit(solution)/shard_map/rd,dhe->hre/dot_general | solution.py:301
  17.1 0.5 fusion.5
  17.6 0.1 pad_maximum_fusion
  17.8 0.0 copy-done
  17.8 0.0 copy-done.1
  17.8 47.2 %exchange.1 = bf16[2,2,128,256]{3,2,1,0:T(8,128)(2,1)S(1)} custom-call(s32[4]{0:T(128)S(1)} %copy-done.1, s32[1]{0:T(128)S(6)} %copy.13.len_ref, bf16[8,4,128,256]{3,2,1,0:T(8,128)(2,1)S(1)} %bitcast.10, bf16[4,128,4096]{2,1,0:T(8,128)(2,1)S(1)} %copy-done, f32[2,128,128]{2,1,0:T(8,128)S(1)} %get-tuple-element.8.cos_ref, ...), custom_call_target="tpu_custom_call" | custom-call | tf_op jit(solution)/shard_map/exchange/pallas_call | solution.py:310
  65.0 1.0 %copy.8 = bf16[2,128,2,256]{3,2,1,0:T(2,128)(2,1)} copy(bf16[2,128,2,256]{3,1,2,0:T(8,128)(2,1)S(1)} %bitcast.11) | data formatting | bytes 524288 | tf_op jit(solution)/shard_map/transpose | solution.py:336
  (2 shorter events, 0.0 us)
Async XLA Ops:
  3.7 14.1 %copy-start = (bf16[4,128,4096]{2,1,0:T(8,128)(2,1)S(1)}, bf16[4,128,4096]{2,1,0:T(8,128)(2,1)}, u32[]{:S(2)}) copy-start(bf16[4,128,4096]{2,1,0:T(8,128)(2,1)} %hidden_ref.1) | copy-start | bytes 12582916
  3.7 14.1 %copy-start.1 = (s32[4]{0:T(128)S(1)}, s32[4]{0:T(128)}, u32[]{:S(2)}) copy-start(s32[4]{0:T(128)} %dest_ref.1) | copy-start | bytes 52

commit v3 on v2

--- a/solution.py
+++ b/solution.py
@@ -2,6 +2,7 @@
 
 import jax
 import jax.numpy as jnp
+import numpy as np
 from jax import lax
 from jax.experimental import pallas as pl
 from jax.experimental.pallas import tpu as pltpu
@@ -14,9 +15,9 @@
 
 def exchange_kernel(
     groups, tps, own, heads, width,
-    dest_ref, len_ref, part_ref, hidden_ref, cos_ref, sin_ref,
+    dest_ref, len_ref, start_ref, part_ref, hidden_ref, freq_ref,
     out_ref,
-    sent, got, mixed, final, mark_s, mark_r, square_s, square_r, sums_s, sums_r, slot_sums, scales,
+    sent, got, mixed, final, mark_s, mark_r, square_s, square_r, sums_s, sums_r, slot_sums, scales, cos_ref, sin_ref,
     s_send, s_recv, c_send, c_recv, m_send, m_recv, r_send, r_recv, q_send, q_recv,
 ):
     g = lax.axis_index("grp")
@@ -113,10 +114,7 @@
 
     mine, _ = slot_of(g)
 
-    @functools.partial(over, tps)
-    def _(i):
-        t = tp_peer(i)
-
+    def send_blocks(t):
         @functools.partial(over, units)
         def _(u):
             head = t * heads + lax.div(u, cuts)
@@ -131,6 +129,36 @@
 
             got[t, u, g] = part_ref[head, mine, span, :]
 
+    send_blocks(tp_peer(0))
+
+    lanes = HD
+    step = 16
+
+    @functools.partial(over, slots * (blk // step))
+    def _(n):
+        s = lax.div(n, blk // step)
+        span = pl.ds(pl.multiple_of(lax.rem(n, blk // step) * step, step), step)
+        totals = [jnp.zeros((step, lanes), jnp.float32)] * 2
+        for c in range(width // lanes):
+            x = hidden_ref[s, span, c * lanes : (c + 1) * lanes].astype(jnp.float32)
+            totals[c % 2] = totals[c % 2] + x * x
+        slot_sums[s, span, :] = totals[0] + totals[1]
+
+    def squares_of(owner):
+        index, _ = slot_of(owner)
+        line = jnp.sum(jnp.transpose(slot_sums[index]), axis=0, keepdims=True)
+        return jnp.broadcast_to(jnp.concatenate([line, line], axis=1), (8, wide))
+
+    square_r[g] = squares_of(g)
+
+    @functools.partial(over, groups - 1)
+    def _(k):
+        o = grp_peer(k)
+        square_s[o] = squares_of(o)
+        square_copy(o, g).start()
+
+    send_blocks(tp_peer(1))
+
     @functools.partial(over, groups - 1)
     def _(k):
         o = grp_peer(k)
@@ -158,33 +186,19 @@
             shard_copy(t, u, z).start()
 
     mix_and_send(tp_peer(0))
-
-    lanes = HD
-
-    @functools.partial(over, slots)
-    def _(s):
-        for r in range(0, blk, 32):
-            def add(c, total):
-                span = pl.ds(pl.multiple_of(c * lanes, lanes), lanes)
-                x = hidden_ref[s, r : r + 32, span].astype(jnp.float32)
-                return total + x * x
-
-            slot_sums[s, r : r + 32, :] = lax.fori_loop(
-                0, width // lanes, add, jnp.zeros((32, lanes), jnp.float32)
-            )
-
-    def squares_of(owner):
-        index, _ = slot_of(owner)
-        line = jnp.sum(jnp.transpose(slot_sums[index]), axis=0, keepdims=True)
-        return jnp.broadcast_to(jnp.concatenate([line, line], axis=1), (8, wide))
-
-    square_r[g] = squares_of(g)
-
-    @functools.partial(over, groups - 1)
-    def _(k):
-        o = grp_peer(k)
-        square_s[o] = squares_of(o)
-        square_copy(o, g).start()
+    band = 32
+    lane = lax.broadcasted_iota(jnp.int32, (band, HD), 1)
+    offset = lax.broadcasted_iota(jnp.int32, (band, HD), 0)
+
+    @functools.partial(over, own * (blk // band))
+    def _(n):
+        j = lax.div(n, blk // band)
+        span = pl.ds(pl.multiple_of(lax.rem(n, blk // band) * band, band), band)
+        positions = (offset + (start_ref[0] + n * band)).astype(jnp.float32)
+        angles = positions * jnp.broadcast_to(freq_ref[0:1, :], (band, HD))
+        sine = jnp.sin(angles)
+        cos_ref[j, span, :] = jnp.cos(angles)
+        sin_ref[j, span, :] = jnp.where(lane < HD // 2, -sine, sine)
 
     @functools.partial(over, groups - 1)
     def _(k):
@@ -204,6 +218,7 @@
 
     @functools.partial(over, tps - 2)
     def _(i):
+        send_blocks(tp_peer(i + 2))
         mix_and_send(tp_peer(i + 1))
 
     @functools.partial(over, units)
@@ -276,17 +291,10 @@
             shard_copy(t, u, z).wait_send()
 
 
-def rotation(start, own, blk):
+def frequencies():
     half = HD // 2
-    steps = jnp.arange(half).astype(jnp.float32)
-    freqs = jnp.exp(-jnp.log(jnp.float32(500000.0)) * (2.0 * steps / HD))
-    positions = start[0] + jnp.arange(own * blk)
-    angles = positions.astype(jnp.float32)[:, None] * freqs[None, :]
-    cosine, sine = jnp.cos(angles), jnp.sin(angles)
-    return (
-        jnp.concatenate([cosine, cosine], axis=1).reshape(own, blk, HD),
-        jnp.concatenate([-sine, sine], axis=1).reshape(own, blk, HD),
-    )
+    freqs = np.exp(-np.log(500000.0) * (2.0 * np.arange(half) / HD))
+    return jnp.asarray(np.tile(np.concatenate([freqs, freqs]), (8, 1)).astype(np.float32))
 
 
 def body(hidden, norm_gain, kv_weight, dest_slot, session_len, session_start):
@@ -295,22 +303,22 @@
     own = (3 * groups + 7) // 8
     heads = kv_weight.shape[1] // tps
     wide_cols = kv_weight.shape[2]
-    cosine, sine = rotation(session_start, own, blk)
     wide = hidden.astype(jnp.float32)
     scaled = (wide * norm_gain[None, None, :]).astype(jnp.bfloat16).reshape(slots * blk, width)
     parts = jnp.einsum("rd,dhe->hre", scaled, kv_weight, preferred_element_type=jnp.float32)
     parts = parts.astype(jnp.bfloat16).reshape(kv_weight.shape[1], slots, blk, wide_cols)
     vmem = pl.BlockSpec(memory_space=pltpu.VMEM)
     smem = pl.BlockSpec(memory_space=pltpu.SMEM)
-    cuts = 2
+    cuts = 1
     units = heads * cuts
     piece = (blk // cuts, wide_cols)
     line = pltpu.VMEM((groups, 8, wide_cols), jnp.float32)
+    table = pltpu.VMEM((own, blk, HD), jnp.float32)
     dma = pltpu.SemaphoreType.DMA
     out = pl.pallas_call(
         functools.partial(exchange_kernel, groups, tps, own, heads, width),
         out_shape=jax.ShapeDtypeStruct((own, heads, blk, wide_cols), jnp.bfloat16),
-        in_specs=[smem, smem, vmem, vmem, vmem, vmem],
+        in_specs=[smem, smem, smem, vmem, vmem, vmem],
         out_specs=vmem,
         scratch_shapes=[
             pltpu.VMEM((tps, units, groups) + piece, jnp.bfloat16),
@@ -321,7 +329,7 @@
             pltpu.VMEM((8, wide_cols), jnp.float32),
             pltpu.VMEM((tps, 8, wide_cols), jnp.float32),
             pltpu.VMEM((slots, blk, HD), jnp.float32),
-            pltpu.VMEM((own, blk, HD), jnp.float32),
+            table, table, table,
             dma((tps, units, groups)), dma((tps, units, groups)),
             dma((tps, units)), dma((tps, units)),
             dma((groups,)), dma((groups,)),
@@ -332,7 +340,7 @@
             collective_id=0, has_side_effects=True, vmem_limit_bytes=40 * 1024 * 1024
         ),
         name="exchange",
-    )(dest_slot, session_len, parts, hidden, cosine, sine)
+    )(dest_slot, session_len, session_start, parts, hidden, frequencies())
     return jnp.transpose(out, (0, 2, 1, 3))
 
 

time: 66.1 us -> 55.6 us (0.84)
  Pallas kernels: 47.2 us -> 37.4 us
  other arithmetic: 3.74 us -> 3.05 us
    pallas_call x1, Pallas kernels: 47.2 us -> 37.4 us  [body(): pl.pallas_call(functools.partial(exchange_kernel, groups, tps, own, heads...]
where the time goes in v3:
time: 55.6 us; the launch traced here: 55.4 us
  Pallas kernels  37.4 us (67%)
  matrix products  12.7 us (23%)
  other arithmetic  3.05 us (5%)
  between operations  1.37 us (2%)
  local copies, waits for them, and re-layouts  0.99 us (2%)
    pallas_call x1, Pallas kernels, body(): pl.pallas_call(functools.partial(exchange_kernel, groups, tps, own, heads...  37.4 us
    dot_general x1, matrix products, body(): jnp.einsum('rd,dhe->hre', scaled, kv_weight, preferred_element_type=jnp.f...  12.7 us
    convert_element_type x1, other arithmetic, body(): (wide * norm_gain[None, None, :]).astype(jnp.bfloat16)  3.05 us

profile of v3, /device:TPU:0, one launch (start us, length us, event | category | flops | bytes accessed | tf_op | source)
XLA Modules:
  0.0 55.4 jit_solution(10554603451624385776)
XLA Ops:
  0.0 3.1 %multiply_convert_fusion = bf16[4,128,4096]{2,1,0:T(8,128)(2,1)S(1)} fusion(bf16[4,128,4096]{2,1,0:T(8,128)(2,1)} %hidden_ref.1, f32[4096]{0:T(1024)} %param.8), kind=kLoop, calls=%fused_computation.2 | loop fusion | flops 6291456 | bytes 8404992 | tf_op jit(solution)/shard_map/convert_element_type | solution.py:307
  3.1 0.0 copy-start
  3.1 0.0 copy-start.1
  3.1 0.0 copy-start.2
  3.1 12.7 %fusion.2 = bf16[512,8,256]{2,0,1:T(8,128)(2,1)S(1)} fusion(bf16[512,4096,1]{1,0,2:T(8,128)(2,1)S(1)} %bitcast.10, bf16[4096,8,256]{2,1,0:T(8,128)(2,1)} %param.9), kind=kOutput, calls=%fused_computation.3 | convolution fusion | flops 8590983168 | bytes 23068672 | tf_op jit(solution)/shard_map/rd,dhe->hre/dot_general | solution.py:308
  17.1 0.0 copy-done
  17.1 0.0 copy-done.1
  17.1 0.0 copy-done.2
  17.1 37.4 %exchange.1 = bf16[2,2,128,256]{3,2,1,0:T(8,128)(2,1)S(1)} custom-call(s32[4]{0:T(128)S(1)} %copy-done.2, s32[1]{0:T(128)S(6)} %copy.14.len_ref, s32[1]{0:T(128)S(6)} %copy.15.start_ref, bf16[8,4,128,256]{3,2,1,0:T(8,128)(2,1)S(1)} %bitcast.8, bf16[4,128,4096]{2,1,0:T(8,128)(2,1)S(1)} %copy-done, f32[8,128]{1,0:T(8,128)S(1)} %copy-done.1), custom_call_target="tpu_custom_call" | custom-call | tf_op jit(solution)/shard_map/exchange/pallas_call | solution.py:318
  54.5 1.0 %copy.9 = bf16[2,128,2,256]{3,2,1,0:T(2,128)(2,1)} copy(bf16[2,128,2,256]{3,1,2,0:T(8,128)(2,1)S(1)} %bitcast.9) | data formatting | bytes 524288 | tf_op jit(solution)/shard_map/transpose | solution.py:344
Async XLA Ops:
  3.1 14.0 %copy-start = (bf16[4,128,4096]{2,1,0:T(8,128)(2,1)S(1)}, bf16[4,128,4096]{2,1,0:T(8,128)(2,1)}, u32[]{:S(2)}) copy-start(bf16[4,128,4096]{2,1,0:T(8,128)(2,1)} %hidden_ref.1) | copy-start | bytes 12582916
  3.1 14.0 %copy-start.1 = (f32[8,128]{1,0:T(8,128)S(1)}, f32[8,128]{1,0:T(8,128)}, u32[]{:S(2)}) copy-start(f32[8,128]{1,0:T(8,128)} %constant.2.clone.freq_ref) | copy-start | bytes 12292
  3.1 14.0 %copy-start.2 = (s32[4]{0:T(128)S(1)}, s32[4]{0:T(128)}, u32[]{:S(2)}) copy-start(s32[4]{0:T(128)} %dest_ref.1) | copy-start | bytes 52

commit v4 on v3

--- a/solution.py
+++ b/solution.py
@@ -33,7 +33,8 @@
         lax.fori_loop(0, n, lambda i, c: (body(i), c)[1], 0)
 
     def grp_peer(k):
-        return lax.rem(g + k + 1, groups)
+        pair = lax.rem(lax.div(g, 2) + 1 + lax.div(k, 2), groups // 2)
+        return 2 * pair + lax.rem(g + 1 + k, 2)
 
     def tp_peer(k):
         side = lax.div(k + 1, 2) * (2 * lax.rem(k, 2) - 1)

time: 55.6 us -> 54.9 us (0.987)
  Pallas kernels: 37.4 us -> 36.6 us
    pallas_call x1, Pallas kernels: 37.4 us -> 36.6 us  [body(): pl.pallas_call(functools.partial(exchange_kernel, groups, tps, own, heads...]
where the time goes in v4:
time: 54.9 us; the launch traced here: 54.7 us
  Pallas kernels  36.6 us (67%)
  matrix products  12.7 us (23%)
  other arithmetic  3.05 us (6%)
  between operations  1.37 us (2%)
  local copies, waits for them, and re-layouts  0.99 us (2%)
    pallas_call x1, Pallas kernels, body(): pl.pallas_call(functools.partial(exchange_kernel, groups, tps, own, heads...  36.6 us
    dot_general x1, matrix products, body(): jnp.einsum('rd,dhe->hre', scaled, kv_weight, preferred_element_type=jnp.f...  12.7 us
    convert_element_type x1, other arithmetic, body(): (wide * norm_gain[None, None, :]).astype(jnp.bfloat16)  3.05 us

profile of v4, /device:TPU:0, one launch (start us, length us, event | category | flops | bytes accessed | tf_op | source)
XLA Modules:
  0.0 54.7 jit_solution(12923483177104982060)
XLA Ops:
  0.0 3.1 %multiply_convert_fusion = bf16[4,128,4096]{2,1,0:T(8,128)(2,1)S(1)} fusion(bf16[4,128,4096]{2,1,0:T(8,128)(2,1)} %hidden_ref.1, f32[4096]{0:T(1024)} %param.8), kind=kLoop, calls=%fused_computation.2 | loop fusion | flops 6291456 | bytes 8404992 | tf_op jit(solution)/shard_map/convert_element_type | solution.py:308
  3.1 0.0 copy-start
  3.1 0.0 copy-start.1
  3.1 0.0 copy-start.2
  3.1 12.7 %fusion.2 = bf16[512,8,256]{2,0,1:T(8,128)(2,1)S(1)} fusion(bf16[512,4096,1]{1,0,2:T(8,128)(2,1)S(1)} %bitcast.10, bf16[4096,8,256]{2,1,0:T(8,128)(2,1)} %param.9), kind=kOutput, calls=%fused_computation.3 | convolution fusion | flops 8590983168 | bytes 23068672 | tf_op jit(solution)/shard_map/rd,dhe->hre/dot_general | solution.py:309
  17.1 0.0 copy-done
  17.1 0.0 copy-done.1
  17.1 0.0 copy-done.2
  17.1 36.6 %exchange.1 = bf16[2,2,128,256]{3,2,1,0:T(8,128)(2,1)S(1)} custom-call(s32[4]{0:T(128)S(1)} %copy-done.2, s32[1]{0:T(128)S(6)} %copy.14.len_ref, s32[1]{0:T(128)S(6)} %copy.15.start_ref, bf16[8,4,128,256]{3,2,1,0:T(8,128)(2,1)S(1)} %bitcast.8, bf16[4,128,4096]{2,1,0:T(8,128)(2,1)S(1)} %copy-done, f32[8,128]{1,0:T(8,128)S(1)} %copy-done.1), custom_call_target="tpu_custom_call" | custom-call | tf_op jit(solution)/shard_map/exchange/pallas_call | solution.py:319
  53.7 1.0 %copy.9 = bf16[2,128,2,256]{3,2,1,0:T(2,128)(2,1)} copy(bf16[2,128,2,256]{3,1,2,0:T(8,128)(2,1)S(1)} %bitcast.9) | data formatting | bytes 524288 | tf_op jit(solution)/shard_map/transpose | solution.py:345
Async XLA Ops:
  3.1 14.0 %copy-start = (bf16[4,128,4096]{2,1,0:T(8,128)(2,1)S(1)}, bf16[4,128,4096]{2,1,0:T(8,128)(2,1)}, u32[]{:S(2)}) copy-start(bf16[4,128,4096]{2,1,0:T(8,128)(2,1)} %hidden_ref.1) | copy-start | bytes 12582916
  3.1 14.0 %copy-start.1 = (f32[8,128]{1,0:T(8,128)S(1)}, f32[8,128]{1,0:T(8,128)}, u32[]{:S(2)}) copy-start(f32[8,128]{1,0:T(8,128)} %constant.2.clone.freq_ref) | copy-start | bytes 12292
  3.1 14.0 %copy-start.2 = (s32[4]{0:T(128)S(1)}, s32[4]{0:T(128)}, u32[]{:S(2)}) copy-start(s32[4]{0:T(128)} %dest_ref.1) | copy-start | bytes 52
